TPU v7x, 32 devices: a whole 2x2x4 slice. The times are simulated.
32 devices in a mesh: pb: 4 (over z), pa: 8 (over y, x, core).
Axes of the slice: x: 2, y: 2, z: 4, core: 2. Of those that a mesh axis runs over, the one named last changes fastest.
Arguments:
- queries: bfloat16 [8192, 1024], P('pb'), may hold values from -16 to 16
- passages: bfloat16 [16384, 1024], P('pa'), may hold values from -5 to 5
- teacher: float32 [8192, 4096], P('pb', 'pa'), may hold values from -20 to 300
- block_ids: int32 [64, 32], P('pb', 'pa'), may hold values from 0 to 127, as said below
Outputs:
- loss: float32 [8192], P(('pb', 'pa'))
- grad_queries: float32 [8192, 1024], P(('pb', 'pa'))
- grad_passages: float32 [16384, 1024], P(('pa', 'pb'))
Inputs may be any that keep to these rules, and one draw needn't show every extreme that they name: Block g belongs to passage shard g // 16. Among the 64 entries of one device's tile of block_ids (rows of one index of pb, columns of one index of pa), at most 16 name blocks of one shard, and in every tile some shard is named exactly 16 times. The 4 entries of one row of a tile name blocks of different shards.
All inputs are finite; a program needn't handle non-finite values.
Results may differ from a plain program's by a relative error of at most 0.0024.
Values sent between devices are 32-bit elements; how exact they have to be, the bound alone decides.
A program may use at most 192 MiB of HBM per device.

v0:
```python
import math

import jax
import jax.numpy as jnp
from jax import lax
from jax.sharding import PartitionSpec as P

D = 1024
BLOCK = 128
PBLOCKS_DEV = 16


loss_scale = 1024.0


def joined(array, axis, combine):
    everything = jax.tree.map(lambda part: lax.all_gather(part, axis), array)
    initial = jax.tree.map(lambda part: part[0], everything)

    def turn(k, so_far):
        return combine(so_far, jax.tree.map(lambda part: part[k], everything))

    return lax.fori_loop(1, lax.axis_size(axis), turn, initial)


def combine_stats(first, second):
    max_first, sum_first, tmax_first, tsum_first = first
    max_second, sum_second, tmax_second, tsum_second = second
    both_max = jnp.maximum(max_first, max_second)
    both_tmax = jnp.maximum(tmax_first, tmax_second)
    total = sum_first * jnp.exp(max_first - both_max) + sum_second * jnp.exp(max_second - both_max)
    teacher_total = tsum_first * jnp.exp(tmax_first - both_tmax) + tsum_second * jnp.exp(
        tmax_second - both_tmax
    )
    return (both_max, total, both_tmax, teacher_total)


def pack_tiles(source, block_ids, pa_count):
    qblock_count, slots_here = block_ids.shape
    entries = qblock_count * slots_here
    capacity = 2 * ((entries + pa_count - 1) // pa_count)
    flat_ids = block_ids.reshape(entries)
    owners = flat_ids // PBLOCKS_DEV
    local_block = flat_ids % PBLOCKS_DEV
    entry_order = jnp.arange(entries, dtype=jnp.int32)
    same_owner = (owners[:, None] == owners[None, :]) & (
        entry_order[None, :] < entry_order[:, None]
    )
    slot_rank = jnp.sum(same_owner.astype(jnp.int32), axis=1)
    destination = owners * capacity + slot_rank
    onehot = destination[None, :] == jnp.arange(pa_count * capacity, dtype=jnp.int32)[:, None]
    tile_data = source.reshape(qblock_count, BLOCK, slots_here, BLOCK).transpose(0, 2, 1, 3)
    tile_data = tile_data.reshape(entries, BLOCK * BLOCK)
    packed = jnp.dot(
        onehot.astype(jnp.float32),
        tile_data,
        precision=lax.Precision.HIGHEST,
        preferred_element_type=jnp.float32,
    )
    meta_marks = jnp.stack([entry_order // slots_here + 1, local_block + 1], axis=1)
    tile_meta = jnp.sum(onehot.astype(jnp.int32)[:, :, None] * meta_marks[None, :, :], axis=1) - 1
    return (
        packed.reshape(pa_count, capacity, BLOCK * BLOCK),
        tile_meta.reshape(pa_count, capacity, 2),
    )


def per_device(queries, passages, teacher, block_ids):
    query_count = queries.shape[0]
    passage_count = passages.shape[0]
    qblock_count = query_count // BLOCK
    pblock_count = passage_count // BLOCK
    pa_count = lax.axis_size("pa")
    score_scale = 2.0 / math.sqrt(D)
    scores = (
        lax.dot_general(
            queries, passages, (((1,), (1,)), ((), ())), preferred_element_type=jnp.float32
        )
        * score_scale
    )
    row_max = jnp.max(scores, axis=1)
    row_sum = jnp.sum(jnp.exp(scores - row_max[:, None]), axis=1)
    teacher_max = jnp.max(teacher, axis=1)
    teacher_sum = jnp.sum(jnp.exp(teacher - teacher_max[:, None]), axis=1)
    whole_max, whole_sum, whole_tmax, whole_tsum = joined(
        (row_max, row_sum, teacher_max, teacher_sum), "pa", combine_stats
    )
    lse_student = whole_max + jnp.log(whole_sum)
    lse_teacher = whole_tmax + jnp.log(whole_tsum)
    teacher_probs = jnp.exp(teacher - lse_teacher[:, None])
    packed, tile_meta = pack_tiles(teacher_probs, block_ids, pa_count)
    got_tiles, got_meta = (
        lax.all_to_all(packed, "pa", split_axis=0, concat_axis=0, tiled=True),
        lax.all_to_all(tile_meta, "pa", split_axis=0, concat_axis=0, tiled=True),
    )
    slot_total = got_tiles.shape[0] * got_tiles.shape[1]
    flat_tiles = got_tiles.reshape(slot_total, BLOCK * BLOCK)
    flat_meta = got_meta.reshape(slot_total, 2)
    row_block = flat_meta[:, 0]
    col_block = flat_meta[:, 1]
    live_slot = col_block >= 0
    flat_tiles = jnp.where(live_slot[:, None], flat_tiles, 0.0)
    target = jnp.where(live_slot, row_block * pblock_count + col_block, -1)
    place = (
        jnp.arange(qblock_count * pblock_count, dtype=jnp.int32)[:, None] == target[None, :]
    ).astype(jnp.float32)
    listed = jnp.dot(
        place, flat_tiles, precision=lax.Precision.HIGHEST, preferred_element_type=jnp.float32
    )
    listed = listed.reshape(qblock_count, pblock_count, BLOCK, BLOCK).transpose(0, 2, 1, 3)
    listed = listed.reshape(query_count, passage_count)
    hard_rows = jnp.sum(listed * scores, axis=1)
    weights = jnp.exp(scores - lse_student[:, None]) - listed
    dscore = (weights * (loss_scale * score_scale)).astype(jnp.bfloat16)
    loss_part = jnp.sum(teacher_probs * (teacher - lse_teacher[:, None]), axis=1) - hard_rows
    query_part = jnp.dot(dscore, passages, preferred_element_type=jnp.float32)
    grad_queries, loss_sum = (
        lax.psum_scatter(query_part, "pa", scatter_dimension=0, tiled=True),
        lax.psum_scatter(loss_part, "pa", scatter_dimension=0, tiled=True),
    )
    row_count = query_count // pa_count
    first_row = lax.axis_index("pa") * row_count
    loss_rows = loss_sum + lax.dynamic_slice_in_dim(lse_student, first_row, row_count)
    grad_passages = lax.psum_scatter(
        lax.dot_general(
            dscore, queries, (((0,), (0,)), ((), ())), preferred_element_type=jnp.float32
        ),
        "pb",
        scatter_dimension=0,
        tiled=True,
    )
    return (loss_rows, grad_queries, grad_passages)


def solution(mesh):
    in_specs = (P("pb", None), P("pa", None), P("pb", "pa"), P("pb", "pa"))
    out_specs = (P(("pb", "pa")), P(("pb", "pa"), None), P(("pa", "pb"), None))
    return jax.shard_map(
        per_device, mesh=mesh, in_specs=in_specs, out_specs=out_specs, check_vma=False
    )
```

profile of v0, /device:TPU:16, one launch (start us, length us, event | category | flops | bytes accessed | tf_op | source)
XLA Modules:
  0.0 515.4 jit_solution(7460800331349548786)
XLA Ops:
  7.2 0.8 copy.33
  7.9 0.1 reshape.277
  8.0 0.1 reshape.278
  8.1 0.2 convert_reduce_fusion
  8.3 0.1 fusion.10
  8.4 0.1 multiply_reduce_fusion.3
  8.5 0.1 sub.107
  8.6 0.6 copy.35
  9.2 3.7 all-to-all-start
  12.9 2.5 reduce_max.19
  15.5 9.7 %all-gather.2 = f32[16384]{0:T(1024)S(1)} all-gather(f32[2048]{0:T(1024)S(1)} %reduce_max.19), channel_id=4, replica_groups=mesh['pb'=4,'pa'=8] {'pa'}, dimensions={0}, use_global_device_ids=true | all-gather | bytes 73728 | tf_op jit(solution)/shard_map/all_gather | solution.py:17
  25.2 3.3 exponential_reduce_fusion.1
  28.5 15.2 %multiply_reduce_fusion.1 = (f32[2048]{0:T(1024)S(1)}, f32[2048,2048]{0,1:T(8,128)}) fusion(bf16[2048,1024]{1,0:T(8,128)(2,1)} %param.6, bf16[2048,1024]{1,0:T(8,128)(2,1)} %param.7), kind=kOutput, calls=%fused_computation.10 | convolution fusion | flops 8598321152 | bytes 25174016 | tf_op jit(solution)/shard_map/dot_general | solution.py:76
  43.7 9.2 %all-gather = f32[16384]{0:T(1024)S(1)} all-gather(f32[2048]{0:T(1024)S(1)} %get-tuple-element.258), channel_id=2, replica_groups=mesh['pb'=4,'pa'=8] {'pa'}, dimensions={0}, use_global_device_ids=true | all-gather | bytes 73728 | tf_op jit(solution)/shard_map/all_gather | solution.py:17
  52.9 8.6 %exponential_reduce_fusion = f32[2048]{0:T(1024)S(1)} fusion(f32[2048,2048]{0,1:T(8,128)} %get-tuple-element.259, f32[2048]{0:T(1024)S(1)} %get-tuple-element.258), kind=kLoop, calls=%fused_computation.9 | loop fusion | flops 12580864 | bytes 16793600 | tf_op jit(solution)/shard_map/reduce_sum | solution.py:82
  61.4 8.3 %all-gather.1 = f32[16384]{0:T(1024)S(1)} all-gather(f32[2048]{0:T(1024)S(1)} %exponential_reduce_fusion), channel_id=3, replica_groups=mesh['pb'=4,'pa'=8] {'pa'}, dimensions={0}, use_global_device_ids=true | all-gather | bytes 73728 | tf_op jit(solution)/shard_map/all_gather | solution.py:17
  69.8 9.4 %all-gather.3 = f32[16384]{0:T(1024)S(1)} all-gather(f32[2048]{0:T(1024)S(1)} %exponential_reduce_fusion.1), channel_id=5, replica_groups=mesh['pb'=4,'pa'=8] {'pa'}, dimensions={0}, use_global_device_ids=true | all-gather | bytes 73728 | tf_op jit(solution)/shard_map/all_gather | solution.py:17
  79.2 0.9 while.21
  80.1 5.2 %subtract_exponential_fusion = (f32[2048,512]{1,0:T(8,128)}, f32[2048]{0:T(1024)S(1)}) fusion(f32[2048,512]{1,0:T(8,128)} %param.8, f32[2048]{0:T(1024)S(1)} %get-tuple-element.261), kind=kLoop, calls=%fused_computation.14 | loop fusion | flops 3143680 | bytes 8404992 | tf_op jit(solution)/shard_map/exp | solution.py:90
  85.3 5.2 %reshape.280 = f32[16,128,4,128]{3,2,1,0:T(4,128)} reshape(f32[2048,512]{1,0:T(8,128)} %get-tuple-element.256) | data formatting | bytes 8388608 | tf_op jit(solution)/shard_map/reshape | solution.py:52
  90.5 4.8 copy.37
  95.3 4.9 reshape.296
  100.2 8.4 %fusion.5 = f32[8,16,16384]{2,1,0:T(8,128)} fusion(f32[64,16384,1]{1,0,2:T(8,128)} %reshape.296, s32[8,16]{1,0:T(8,128)S(1)} %multiply_add_fusion.3, s32[64]{0:T(128)S(1)} %multiply_add_fusion.4), kind=kOutput, calls=%fused_computation.21 | convolution fusion | flops 1610620928 | bytes 12583680 | tf_op jit(solution)/shard_map/dot_general | solution.py:54
  108.6 0.0 all-to-all-done
  108.6 5.0 all-to-all-start.1
  113.6 0.0 reduce-scatter.3.cloned.1.call-start
  113.7 0.1 reshape.279
  113.8 93.9 %all-to-all-done.1 = f32[8,16,16384]{2,1,0:T(8,128)} async-done(((f32[8,16,16384]{2,1,0:T(8,128)}), f32[8,16,16384]{2,1,0:T(8,128)}, u32[]{:S(2)}, u32[]{:S(2)}) %all-to-all-start.1) | async-done | bytes 8388640 | tf_op jit(solution)/shard_map/all_to_all | solution.py:93
  207.7 7.5 %bitcast_select_fusion = f32[128,16384]{1,0:T(8,128)} fusion(f32[8,16,16384]{2,1,0:T(8,128)} %all-to-all-done.1, pred[128]{0:T(512)(128)(4,1)S(1)} %compare_bitcast_fusion), kind=kLoop, calls=%fused_computation.11 | loop fusion | flops 2097152 | bytes 16777344 | tf_op jit(solution)/shard_map/jit(_where)/select_n | solution.py:102
  215.2 9.0 %copy.38 = f32[16384,128]{1,0:T(8,128)} copy(f32[16384,128]{0,1:T(8,128)} %bitcast.51) | data formatting | bytes 16777216 | tf_op jit(solution)/shard_map/dot_general | solution.py:107
  224.1 9.6 %fusion = f32[16,16,128,128]{3,1,2,0:T(8,128)S(1)} fusion(f32[128,128,128,1]{2,1,0,3:T(8,128)} %bitcast.52, s32[128]{0:T(128)S(1)} %fusion.12, s32[16,16]{1,0:T(8,128)S(1)} %multiply_add_fusion.2), kind=kOutput, calls=%fused_computation.15 | convolution fusion | flops 6442483712 | bytes 25167360 | tf_op jit(solution)/shard_map/dot_general | solution.py:107
  233.7 11.2 %copy.44 = f32[256,8,16,128]{3,1,2,0:T(8,128)} copy(f32[256,8,16,128]{3,2,1,0:T(8,128)S(1)} %bitcast.49) | data formatting | bytes 33554432
  244.9 17.6 %copy.41 = f32[2048,2048]{0,1:T(8,128)} copy(f32[2048,2048]{1,0:T(8,128)} %bitcast.50) | data formatting | bytes 33554432 | tf_op jit(solution)/shard_map/reshape | solution.py:111
  262.5 0.0 copy-start.1
  262.5 12.3 %multiply_convert_fusion = (bf16[2048,2048]{0,1:T(8,128)(2,1)S(1)}, f32[2048]{0:T(1024)S(1)}) fusion(f32[2048,2048]{0,1:T(8,128)} %copy.41, f32[2048,2048]{0,1:T(8,128)} %get-tuple-element.259, f32[2048]{0:T(1024)S(1)} %get-tuple-element.260), kind=kLoop, calls=%fused_computation.7 | loop fusion | flops 29358080 | bytes 41959424 | tf_op jit(solution)/shard_map/convert_element_type | solution.py:114
  274.8 0.0 copy-start
  274.9 3.2 copy-done
  278.1 0.0 copy-done.1
  278.1 11.5 %fusion.15 = f32[2048,1024]{1,0:T(8,128)} fusion(bf16[2048,2048]{0,1:T(8,128)(2,1)S(1)} %get-tuple-element.254, bf16[2048,1024]{1,0:T(8,128)(2,1)S(1)} %copy-done.1), kind=kOutput, calls=%fused_computation.55 | convolution fusion | flops 8589934592 | bytes 20971520 | tf_op jit(solution)/shard_map/dot_general | solution.py:116
  289.6 0.0 reduce-scatter.3.cloned.1.call-update
  289.6 0.0 reduce-scatter.5.cloned.1.call-start
  289.6 14.7 %fusion.16 = f32[2048,1024]{1,0:T(8,128)} fusion(bf16[2048,2048]{0,1:T(8,128)(2,1)} %copy-done, bf16[2048,1024]{1,0:T(8,128)(2,1)} %param.6), kind=kOutput, calls=%fused_computation.56 | convolution fusion | flops 8589934592 | bytes 20971520 | tf_op jit(solution)/shard_map/dot_general | solution.py:125
  304.3 0.0 copy-start.2
  304.3 0.0 reduce-scatter.5.cloned.1.call-update
  304.3 0.6 copy-done.2
  304.9 0.6 dynamic-slice
  306.2 12.3 %all-reduce = f32[2048]{0:T(1024)S(1)} all-reduce(f32[2048]{0:T(1024)S(1)} %sub.108), channel_id=6, replica_groups=mesh['pb'=4,'pa'=8] {'pa'}, use_global_device_ids=true, to_apply=%region_10.11.clone | all-reduce | flops 2048 | bytes 16384
  318.5 0.6 dynamic-slice_add_fusion
  319.2 41.2 %reduce-scatter.3.cloned.1.call-done = f32[256,1024]{1,0:T(8,128)} async-done(((f32[2048,1024]{1,0:T(8,128)}), f32[256,1024]{1,0:T(8,128)}) %reduce-scatter.3.cloned.1.call-update) | async-done | bytes 1048592 | tf_op jit(solution)/shard_map/reduce_scatter | solution.py:118
  360.3 148.3 %reduce-scatter.5.cloned.1.call-done = f32[512,1024]{1,0:T(8,128)} async-done(((f32[2048,1024]{1,0:T(8,128)}), f32[512,1024]{1,0:T(8,128)}) %reduce-scatter.5.cloned.1.call-update) | async-done | bytes 2097168 | tf_op jit(solution)/shard_map/reduce_scatter | solution.py:124
  (55 shorter events, 0.7 us)
Async XLA Ops:
  9.2 99.4 %all-to-all-start = ((s32[8,16,2]{1,2,0:T(2,128)}), s32[8,16,2]{1,2,0:T(2,128)S(1)}, u32[]{:S(2)}, u32[]{:S(2)}) async-start(s32[8,16,2]{1,2,0:T(2,128)} %copy.35), calls=%async_computation | async-start | bytes 16384 | tf_op jit(solution)/shard_map/all_to_all | solution.py:94
  108.6 99.0 %all-to-all-start.1 = ((f32[8,16,16384]{2,1,0:T(8,128)}), f32[8,16,16384]{2,1,0:T(8,128)}, u32[]{:S(2)}, u32[]{:S(2)}) async-start(f32[8,16,16384]{2,1,0:T(8,128)} %fusion.5), calls=%async_computation.1 | async-start | bytes 16777216 | tf_op jit(solution)/shard_map/all_to_all | solution.py:93
  113.6 246.7 %reduce-scatter.3.cloned.1.call-start = ((), (), s32[]{:S(2)}) async-start(), calls=%async_computation.4 | async-start | bytes 9437184 | tf_op jit(solution)/shard_map/reduce_scatter | solution.py:118
  262.5 15.5 %copy-start.1 = (bf16[2048,1024]{1,0:T(8,128)(2,1)S(1)}, bf16[2048,1024]{1,0:T(8,128)(2,1)}, u32[]{:S(2)}) copy-start(bf16[2048,1024]{1,0:T(8,128)(2,1)} %param.7) | copy-start | bytes 12582916
  274.8 3.2 copy-start
  289.6 219.0 %reduce-scatter.5.cloned.1.call-start = ((), (), s32[]{:S(2)}) async-start(), calls=%async_computation.5 | async-start | bytes 10485760 | tf_op jit(solution)/shard_map/reduce_scatter | solution.py:124
  304.3 0.7 copy-start.2
Sparse Core Ops, SparseCore 0:
  289.7 70.5 reduce-scatter.2
  363.4 145.1 reduce-scatter.4
where the time goes:
time: 518 us; the launch traced here: 515 us
  waiting for transfers between devices  283 us (55%)
  local copies, waits for them, and re-layouts  59.3 us (11%)
  matrix products  59.3 us (11%)
  blocking collectives  48.9 us (9%)
  other arithmetic  40.6 us (8%)
  between operations  14.9 us (3%)
  starting transfers between devices  8.77 us (2%)
    reduce_scatter x1, waiting for transfers between devices, per_device(): lax.psum_scatter(lax.dot_general(dscore, queries, (((0,), (0,)), ((), ())...  148 us
    all_to_all x1, waiting for transfers between devices, per_device(): lax.all_to_all(packed, 'pa', split_axis=0, concat_axis=0, tiled=True)  93.9 us
    reduce_scatter x1, waiting for transfers between devices, per_device(): lax.psum_scatter(query_part, 'pa', scatter_dimension=0, tiled=True)  41.2 us
    all_gather x4, blocking collectives, joined(): everything = jax.tree.map(lambda part: lax.all_gather(part, axis), array)  36.5 us
    reshape x1, local copies, waits for them, and re-layouts, per_device(): listed = listed.reshape(query_count, passage_count)  17.6 us
    unnamed x9, local copies, waits for them, and re-layouts  16.4 us
    dot_general x1, matrix products, per_device(): lax.dot_general(queries, passages, (((1,), (1,)), ((), ())), preferred_el...  15.2 us
    dot_general x1, matrix products, per_device(): lax.dot_general(dscore, queries, (((0,), (0,)), ((), ())), preferred_elem...  14.7 us
  transfers between devices with their start and end apart: 4, of which 3 were waited for; matrix products, arithmetic and copies ran while one was open for 14% of the time, Pallas kernels for 0%

commit v1 on v0

v1 whole, which is shorter than its diff:
```python
import functools
import math

import jax
import jax.numpy as jnp
from jax import lax
from jax.experimental import pallas as pl
from jax.experimental.pallas import tpu as pltpu
from jax.sharding import PartitionSpec as P

BLOCK = 128
ROWS = 256
MIB = 1024 * 1024
loss_scale = 1024.0


def rows_to_lanes(columns, rows):
    lane = lax.broadcasted_iota(jnp.int32, (rows, BLOCK), 1)
    wide = jnp.zeros((rows, BLOCK), jnp.float32)
    for i, column in enumerate(columns):
        wide = jnp.where(lane == i, column, wide)
    return wide.T[0:8, :]


def pack_kernel(pick_ref, teacher_ref, tiles_ref, stats_ref):
    step = pl.program_id(0)
    rows = teacher_ref.shape[0]
    pa_count = tiles_ref.shape[0]
    for half in range(rows // BLOCK):
        block = step * (rows // BLOCK) + half
        for owner in range(pa_count):
            first = pl.multiple_of(pick_ref[owner, block] * BLOCK, BLOCK)
            tiles_ref[owner, half] = teacher_ref[
                half * BLOCK : (half + 1) * BLOCK, pl.ds(first, BLOCK)
            ]
    values = teacher_ref[...]
    top = jnp.max(values, axis=1, keepdims=True)
    below = values - top
    grown = jnp.exp(below)
    total = jnp.sum(grown, axis=1, keepdims=True)
    moment = jnp.sum(grown * below, axis=1, keepdims=True)
    stats_ref[...] = rows_to_lanes((top, total, moment), rows)


def pack(teacher, pick):
    query_count, width = teacher.shape
    pa_count, qblocks = pick.shape
    return pl.pallas_call(
        pack_kernel,
        grid_spec=pltpu.PrefetchScalarGridSpec(
            num_scalar_prefetch=1,
            grid=(query_count // ROWS,),
            in_specs=[pl.BlockSpec((ROWS, width), lambda i, pick: (i, 0))],
            out_specs=[
                pl.BlockSpec(
                    (pa_count, ROWS // BLOCK, BLOCK, BLOCK), lambda i, pick: (0, i, 0, 0)
                ),
                pl.BlockSpec((8, ROWS), lambda i, pick: (0, i)),
            ],
        ),
        out_shape=[
            jax.ShapeDtypeStruct((pa_count, qblocks, BLOCK, BLOCK), jnp.float32),
            jax.ShapeDtypeStruct((8, query_count), jnp.float32),
        ],
        compiler_params=pltpu.CompilerParams(vmem_limit_bytes=40 * MIB),
        cost_estimate=pl.CostEstimate(
            flops=6 * teacher.size,
            bytes_accessed=4 * (teacher.size + pa_count * qblocks * BLOCK * BLOCK),
            transcendentals=teacher.size,
        ),
        name="pack",
    )(pick, teacher)


def scores_kernel(score_scale, queries_ref, passages_ref, scores_ref, stats_ref):
    scores = (
        lax.dot_general(
            queries_ref[...],
            passages_ref[...],
            (((1,), (1,)), ((), ())),
            preferred_element_type=jnp.float32,
        )
        * score_scale
    )
    scores_ref[...] = scores
    top = jnp.max(scores, axis=1, keepdims=True)
    total = jnp.sum(jnp.exp(scores - top), axis=1, keepdims=True)
    stats_ref[...] = rows_to_lanes((top, total), scores.shape[0])


def score_stats(queries, passages, score_scale):
    query_count, depth = queries.shape
    passage_count = passages.shape[0]
    return pl.pallas_call(
        functools.partial(scores_kernel, score_scale),
        grid=(query_count // ROWS,),
        in_specs=[
            pl.BlockSpec((ROWS, depth), lambda i: (i, 0)),
            pl.BlockSpec((passage_count, depth), lambda i: (0, 0)),
        ],
        out_specs=[
            pl.BlockSpec((ROWS, passage_count), lambda i: (i, 0)),
            pl.BlockSpec((8, ROWS), lambda i: (0, i)),
        ],
        out_shape=[
            jax.ShapeDtypeStruct((query_count, passage_count), jnp.float32),
            jax.ShapeDtypeStruct((8, query_count), jnp.float32),
        ],
        compiler_params=pltpu.CompilerParams(vmem_limit_bytes=40 * MIB),
        cost_estimate=pl.CostEstimate(
            flops=2 * query_count * passage_count * depth,
            bytes_accessed=4 * query_count * passage_count
            + 2 * depth * (query_count + passage_count),
            transcendentals=query_count * passage_count,
        ),
        name="score_stats",
    )(queries, passages)


def dscore_kernel(
    scale, col_ref, scores_ref, lse_ref, tiles_ref, passages_ref, dscore_ref, part_ref, weights
):
    step = pl.program_id(0)
    rows, passage_count = scores_ref.shape
    pa_count = tiles_ref.shape[0]
    chunks, chunk_rows, depth = part_ref.shape
    chunk_rows -= 8
    weights[...] = scale * jnp.exp(scores_ref[...] - lse_ref[:, 0:1])
    hard_parts = []
    for half in range(rows // BLOCK):
        block = step * (rows // BLOCK) + half
        span = slice(half * BLOCK, (half + 1) * BLOCK)
        lse_teacher = lse_ref[span, 1:2]

        def one_source(source, hard):
            col = col_ref[source, block]
            first = pl.multiple_of(jnp.maximum(col, 0) * BLOCK, BLOCK)
            probs = jnp.exp(tiles_ref[source, half] - lse_teacher)
            probs = jnp.where(col >= 0, probs, 0.0)
            place = pl.ds(first, BLOCK)
            weights[span, place] -= scale * probs
            return hard + probs * scores_ref[span, place]

        hard_parts.append(
            jnp.sum(
                lax.fori_loop(
                    0, pa_count, one_source, jnp.zeros((BLOCK, BLOCK), jnp.float32)
                ),
                axis=1,
                keepdims=True,
            )
        )
    hard = rows_to_lanes((jnp.concatenate(hard_parts, axis=0),), rows)
    dscore = weights[...].astype(jnp.bfloat16)
    for m in range(passage_count // BLOCK):
        dscore_ref[m] = dscore[:, m * BLOCK : (m + 1) * BLOCK]
    part = jnp.dot(dscore, passages_ref[...], preferred_element_type=jnp.float32)
    for chunk in range(chunks):
        part_ref[chunk, 0:chunk_rows, :] = part[chunk * chunk_rows : (chunk + 1) * chunk_rows]
        part_ref[chunk, chunk_rows : chunk_rows + 8, :] = jnp.zeros((8, depth), jnp.float32)
        part_ref[chunk, chunk_rows : chunk_rows + 8, 0:rows] = hard


def dscore_and_query_part(scores, lse, tiles, cols, passages, scale):
    query_count, passage_count = scores.shape
    depth = passages.shape[1]
    pa_count, qblocks = cols.shape
    chunk_rows = query_count // pa_count
    chunks = ROWS // chunk_rows
    pblocks = passage_count // BLOCK
    return pl.pallas_call(
        functools.partial(dscore_kernel, scale),
        grid_spec=pltpu.PrefetchScalarGridSpec(
            num_scalar_prefetch=1,
            grid=(query_count // ROWS,),
            in_specs=[
                pl.BlockSpec((ROWS, passage_count), lambda i, cols: (i, 0)),
                pl.BlockSpec((ROWS, 2), lambda i, cols: (i, 0)),
                pl.BlockSpec(
                    (pa_count, ROWS // BLOCK, BLOCK, BLOCK), lambda i, cols: (0, i, 0, 0)
                ),
                pl.BlockSpec((passage_count, depth), lambda i, cols: (0, 0)),
            ],
            out_specs=[
                pl.BlockSpec((pblocks, ROWS, BLOCK), lambda i, cols: (0, i, 0)),
                pl.BlockSpec((chunks, chunk_rows + 8, depth), lambda i, cols: (i, 0, 0)),
            ],
            scratch_shapes=[pltpu.VMEM((ROWS, passage_count), jnp.float32)],
        ),
        out_shape=[
            jax.ShapeDtypeStruct((pblocks, query_count, BLOCK), jnp.bfloat16),
            jax.ShapeDtypeStruct((pa_count, chunk_rows + 8, depth), jnp.float32),
        ],
        compiler_params=pltpu.CompilerParams(vmem_limit_bytes=48 * MIB),
        cost_estimate=pl.CostEstimate(
            flops=2 * query_count * passage_count * depth,
            bytes_accessed=6 * query_count * passage_count + 4 * query_count * depth,
            transcendentals=query_count * passage_count,
        ),
        name="dscore",
    )(cols, scores, lse, tiles, passages)


def passages_kernel(
    count,
    dscore_hbm,
    queries_hbm,
    out_ref,
    dscore,
    queries,
    acc,
    from_below,
    from_above,
    load_sem,
    queries_sem,
    up_send,
    up_recv,
    down_send,
    down_recv,
):
    me = lax.axis_index("pb")
    blocks = dscore.shape[0]
    share = blocks // count
    low = me < count // 2

    def in_order(k):
        return jnp.where(low, blocks - 1 - k, k)

    def load(m):
        return pltpu.make_async_copy(dscore_hbm.at[m], dscore.at[m], load_sem.at[m])

    load_queries = pltpu.make_async_copy(queries_hbm, queries, queries_sem)
    load_queries.start()

    @pl.loop(0, blocks)
    def _(k):
        load(in_order(k)).start()

    barrier = pltpu.get_barrier_semaphore()

    @pl.when(me > 0)
    def _():
        pl.semaphore_signal(
            barrier, inc=1, device_id={"pb": me - 1}, device_id_type=pl.DeviceIdType.MESH
        )

    @pl.when(me < count - 1)
    def _():
        pl.semaphore_signal(
            barrier, inc=1, device_id={"pb": me + 1}, device_id_type=pl.DeviceIdType.MESH
        )

    pl.semaphore_wait(
        barrier, jnp.where(me > 0, 1, 0) + jnp.where(me < count - 1, 1, 0)
    )

    def up(m):
        return pltpu.make_async_remote_copy(
            src_ref=acc.at[m],
            dst_ref=from_below.at[m],
            send_sem=up_send.at[m],
            recv_sem=up_recv.at[m],
            device_id={"pb": me + 1},
            device_id_type=pl.DeviceIdType.MESH,
        )

    def down(m):
        return pltpu.make_async_remote_copy(
            src_ref=acc.at[m],
            dst_ref=from_above.at[m],
            send_sem=down_send.at[m],
            recv_sem=down_recv.at[m],
            device_id={"pb": me - 1},
            device_id_type=pl.DeviceIdType.MESH,
        )

    load_queries.wait()

    @pl.loop(0, blocks)
    def _(k):
        m = in_order(k)
        load(m).wait()
        acc[m] = lax.dot_general(
            dscore[m],
            queries[...],
            (((0,), (0,)), ((), ())),
            preferred_element_type=jnp.float32,
        )

        @pl.when((me == 0) & (m // share > me))
        def _():
            up(m).start()

        @pl.when((me == count - 1) & (m // share < me))
        def _():
            down(m).start()

    @pl.loop(0, blocks)
    def _(k):
        upper = blocks - 1 - k

        @pl.when((me > 0) & (upper // share >= me))
        def _():
            up(upper).wait_recv()
            acc[upper] += from_below[upper]

            @pl.when(upper // share > me)
            def _():
                up(upper).start()

        @pl.when((me < count - 1) & (k // share <= me))
        def _():
            down(k).wait_recv()
            acc[k] += from_above[k]

            @pl.when(k // share < me)
            def _():
                down(k).start()

    for c in range(share):
        out_ref[c * BLOCK : (c + 1) * BLOCK, :] = acc[me * share + c]

    @pl.loop(0, blocks)
    def _(m):
        @pl.when(m // share > me)
        def _():
            up(m).wait_send()

        @pl.when(m // share < me)
        def _():
            down(m).wait_send()


def passage_gradient(dscore, queries, count):
    blocks, query_count, _ = dscore.shape
    depth = queries.shape[1]
    rows = blocks // count * BLOCK
    return pl.pallas_call(
        functools.partial(passages_kernel, count),
        in_specs=[pl.BlockSpec(memory_space=pl.ANY)] * 2,
        out_specs=pl.BlockSpec(memory_space=pltpu.VMEM),
        out_shape=jax.ShapeDtypeStruct((rows, depth), jnp.float32),
        scratch_shapes=[
            pltpu.VMEM((blocks, query_count, BLOCK), jnp.bfloat16),
            pltpu.VMEM((query_count, depth), jnp.bfloat16),
            pltpu.VMEM((blocks, BLOCK, depth), jnp.float32),
            pltpu.VMEM((blocks, BLOCK, depth), jnp.float32),
            pltpu.VMEM((blocks, BLOCK, depth), jnp.float32),
            pltpu.SemaphoreType.DMA((blocks,)),
            pltpu.SemaphoreType.DMA,
            pltpu.SemaphoreType.DMA((blocks,)),
            pltpu.SemaphoreType.DMA((blocks,)),
            pltpu.SemaphoreType.DMA((blocks,)),
            pltpu.SemaphoreType.DMA((blocks,)),
        ],
        compiler_params=pltpu.CompilerParams(
            collective_id=0, has_side_effects=True, vmem_limit_bytes=48 * MIB
        ),
        cost_estimate=pl.CostEstimate(
            flops=2 * query_count * blocks * BLOCK * depth,
            bytes_accessed=200 * MIB,
            transcendentals=0,
        ),
        name="passage_gradient",
    )(dscore, queries)


def per_device(queries, passages, teacher, block_ids):
    query_count, depth = queries.shape
    passage_count = passages.shape[0]
    qblocks, slots = block_ids.shape
    pblocks = passage_count // BLOCK
    pa_count = lax.axis_size("pa")
    pb_count = lax.axis_size("pb")
    me = lax.axis_index("pa")
    score_scale = 2.0 / math.sqrt(depth)

    owners = block_ids // pblocks
    shard = jnp.arange(pa_count, dtype=jnp.int32)
    pick = jnp.sum(
        jnp.where(
            owners[None] == shard[:, None, None], jnp.arange(slots, dtype=jnp.int32), 0
        ),
        axis=2,
    )
    packed, teacher_stats = pack(teacher, pick)
    tiles = lax.all_to_all(packed, "pa", split_axis=0, concat_axis=0, tiled=True)

    scores, student_stats = score_stats(queries, passages, score_scale)
    entries = qblocks * slots
    ids = jnp.pad(
        block_ids.astype(jnp.float32).reshape(1, entries), ((0, 0), (0, query_count - entries))
    )
    mine = jnp.concatenate([student_stats[0:2], teacher_stats[0:3], ids], axis=0)
    every = lax.all_gather(mine, "pa")
    top, total, teacher_top, teacher_total, moment = (every[:, i] for i in range(5))
    whole_top = jnp.max(top, axis=0)
    lse_student = whole_top + jnp.log(jnp.sum(total * jnp.exp(top - whole_top), axis=0))
    whole_teacher = jnp.max(teacher_top, axis=0)
    lse_teacher = whole_teacher + jnp.log(
        jnp.sum(teacher_total * jnp.exp(teacher_top - whole_teacher), axis=0)
    )
    below = teacher_top - lse_teacher
    teacher_part = jnp.sum(jnp.exp(below) * (moment + below * teacher_total), axis=0)
    every_ids = every[:, 5, 0:entries].astype(jnp.int32).reshape(pa_count, qblocks, slots)
    cols = (
        jnp.sum(
            jnp.where(every_ids // pblocks == me, every_ids % pblocks + 1, 0), axis=2
        )
        - 1
    )
    lse = jnp.stack([lse_student, lse_teacher], axis=1)

    dscore, query_part = dscore_and_query_part(
        scores, lse, tiles, cols, passages, loss_scale * score_scale
    )
    summed = lax.psum_scatter(query_part, "pa", scatter_dimension=0, tiled=False)
    grad_passages = passage_gradient(dscore, queries, pb_count)
    row_count = query_count // pa_count
    grad_queries = summed[0:row_count]
    hard = lax.dynamic_slice_in_dim(
        summed[row_count], me * row_count % ROWS, row_count
    )
    loss_rows = (
        lax.dynamic_slice_in_dim(lse_student + teacher_part, me * row_count, row_count) - hard
    )
    return (loss_rows, grad_queries, grad_passages)


def solution(mesh):
    in_specs = (P("pb", None), P("pa", None), P("pb", "pa"), P("pb", "pa"))
    out_specs = (P(("pb", "pa")), P(("pb", "pa"), None), P(("pa", "pb"), None))
    return jax.shard_map(
        per_device, mesh=mesh, in_specs=in_specs, out_specs=out_specs, check_vma=False
    )
```

time: 518 us -> 332 us (0.64)
  waiting for transfers between devices: 283 us -> 0.04 us
  Pallas kernels: 0 us -> 210 us
  matrix products: 59.3 us -> 0 us
  local copies, waits for them, and re-layouts: 59.3 us -> 17.2 us
  other arithmetic: 40.6 us -> 2.14 us
  blocking collectives: 48.9 us -> 79.2 us
    pallas_call x0 -> x4, Pallas kernels: none -> 210 us  [the longest x1 162 us: passage_gradient(): pl.pallas_call(functools.partial(passages_kernel, count), in_specs=[pl.Bl...]
    reduce_scatter x2 -> x1, waiting for transfers between devices: 189 us -> 0.02 us  [per_device(): lax.psum_scatter(query_part, 'pa', scatter_dimension=0, tiled=False)]
    all_to_all x1, waiting for transfers between devices: 93.9 us -> 0.01 us  [per_device(): lax.all_to_all(packed, 'pa', split_axis=0, concat_axis=0, tiled=True)]
    dot_general x5 -> x0, matrix products: 59.3 us -> none  [the longest x1 15.2 us: per_device(): lax.dot_general(queries, passages, (((1,), (1,)), ((), ())), preferred_el...]
    all_gather x4 -> x1, blocking collectives: 36.5 us -> 79.2 us  [per_device(): every = lax.all_gather(mine, 'pa')]
    reshape x6 -> x1, local copies, waits for them, and re-layouts: 28 us -> 0.09 us  [per_device(): block_ids.astype(jnp.float32).reshape(1, entries)]
    convert_element_type x2 -> x1, other arithmetic: 12.4 us -> 0.01 us  [per_device(): every[:, 5, 0:entries].astype(jnp.int32).reshape(pa_count, qblocks, slots)]
    unnamed x1 -> x0, blocking collectives: 12.3 us -> none
  transfers between devices with their start and end apart: 4 -> 2, of which waited for: 3 -> 0; matrix products, arithmetic and copies ran while one was open for 14% -> 0% of each run, Pallas kernels for 0% -> 54%
where the time goes in v1:
time: 332 us; the launch traced here: 328 us
  Pallas kernels  210 us (63%)
  blocking collectives  79.2 us (24%)
  local copies, waits for them, and re-layouts  17.2 us (5%)
  between operations  14.2 us (4%)
  starting transfers between devices  5.08 us (2%)
    pallas_call x1, Pallas kernels, passage_gradient(): pl.pallas_call(functools.partial(passages_kernel, count), in_specs=[pl.Bl...  162 us
    all_gather x1, blocking collectives, per_device(): every = lax.all_gather(mine, 'pa')  79.2 us
    pallas_call x1, Pallas kernels, dscore_and_query_part(): pl.pallas_call(functools.partial(dscore_kernel, scale), grid_spec=pltpu.P...  29.9 us
    pallas_call x1, Pallas kernels, score_stats(): pl.pallas_call(functools.partial(scores_kernel, score_scale), grid=(query...  14.5 us
    unnamed x11, local copies, waits for them, and re-layouts  13.3 us
  transfers between devices with their start and end apart: 2, of which 0 were waited for; matrix products, arithmetic and copies ran while one was open for 0% of the time, Pallas kernels for 54%

profile of v1, /device:TPU:16, one launch (start us, length us, event | category | flops | bytes accessed | tf_op | source)
XLA Modules:
  0.0 328.1 jit_solution(16299525791094876827)
XLA Ops:
  7.2 0.8 add_select_fusion.2
  7.9 0.1 copy.29
  8.0 0.1 select_reduce_fusion
  8.1 0.1 copy.30.pick_ref
  8.2 0.0 copy-start.1
  8.2 2.2 copy-done.1
  10.4 4.0 %pack.1 = (f32[8,16,128,128]{3,2,1,0:T(8,128)S(1)}, f32[8,2048]{1,0:T(8,128)S(1)}) custom-call(s32[8,16]{1,0:T(8,128)S(1)} %copy.30.pick_ref, f32[2048,512]{1,0:T(8,128)S(1)} %copy-done.1), custom_call_target="tpu_custom_call" | custom-call | flops 6291456 | bytes 12582912 | tf_op jit(solution)/shard_map/pack/pallas_call | solution.py:48
  14.4 0.0 copy-start
  14.4 3.2 copy-done
  17.7 5.0 %all-to-all-start = ((f32[8,16,128,128]{3,2,1,0:T(8,128)}), f32[8,16,128,128]{3,2,1,0:T(8,128)}, u32[]{:S(2)}, u32[]{:S(2)}) async-start(f32[8,16,128,128]{3,2,1,0:T(8,128)} %copy-done), calls=%async_computation | async-start | bytes 16777216 | tf_op jit(solution)/shard_map/all_to_all | solution.py:387
  22.7 0.0 reduce-scatter.2.cloned.1.call-start
  22.7 0.1 copy.31
  22.8 0.1 reshape.57
  22.9 0.0 copy-start.2
  22.9 2.2 copy-done.2
  25.1 0.0 copy-start.4
  25.1 2.2 copy-done.4
  27.3 14.5 %score_stats.1 = (f32[2048,2048]{1,0:T(8,128)}, f32[8,2048]{1,0:T(8,128)S(1)}) custom-call(bf16[2048,1024]{1,0:T(8,128)(2,1)S(1)} %copy-done.4, bf16[2048,1024]{1,0:T(8,128)(2,1)S(1)} %copy-done.2), custom_call_target="tpu_custom_call" | custom-call | flops 8589934592 | bytes 25165824 | tf_op jit(solution)/shard_map/score_stats/pallas_call | solution.py:94
  41.8 79.2 %all-gather.1 = f32[8,6,2048]{2,1,0:T(8,128)S(1)} all-gather(f32[1,6,2048]{2,1,0:T(8,128)S(1)} %fusion), channel_id=2, replica_groups=mesh['pb'=4,'pa'=8] {'pa'}, dimensions={0}, use_global_device_ids=true | all-gather | bytes 442368 | tf_op jit(solution)/shard_map/all_gather | solution.py:395
  121.1 0.1 copy.36
  121.2 0.1 fusion.10
  121.2 0.1 copy.37
  121.3 0.3 slice_reduce_fusion.1
  121.6 0.1 fusion.4
  121.8 0.4 copy.38.lse_ref
  122.2 0.0 all-to-all-done.tiles_ref
  122.2 0.0 copy-start.3
  122.2 2.2 copy-done.3
  124.4 29.9 %dscore.1 = (bf16[16,2048,128]{2,1,0:T(8,128)(2,1)}, f32[8,264,1024]{2,1,0:T(8,128)}) custom-call(s32[8,16]{1,0:T(8,128)S(1)} %broadcast_add_fusion.col_ref, f32[2048,2048]{1,0:T(8,128)} %get-tuple-element.11.scores_ref, f32[2048,2]{1,0:T(8,128)S(1)} %copy.38.lse_ref, f32[8,16,128,128]{3,2,1,0:T(8,128)} %all-to-all-done.tiles_ref, ...), custom_call_target="tpu_custom_call" | custom-call | flops 8589934592 | bytes 33554432 | tf_op jit(solution)/shard_map/dscore/pallas_call | solution.py:171
  154.3 0.0 reduce-scatter.2.cloned.1.call-update
  154.3 0.1 fusion.6
  154.4 161.8 %passage_gradient.1 = f32[512,1024]{1,0:T(8,128)S(1)} custom-call(bf16[16,2048,128]{2,1,0:T(8,128)(2,1)} %get-tuple-element.14.dscore_hbm, bf16[2048,1024]{1,0:T(8,128)(2,1)} %queries_hbm.1), custom_call_target="tpu_custom_call" | custom-call | flops 8589934592 | bytes 209715200 | tf_op jit(solution)/shard_map/passage_gradient/pallas_call | solution.py:338
  316.2 0.0 reduce-scatter.2.cloned.1.call-done
  316.2 0.8 slice.51
  317.0 0.6 fusion.14
  317.6 2.3 slice_bitcast_fusion
  319.9 1.3 copy.69
  (10 shorter events, 0.1 us)
Async XLA Ops:
  8.2 2.2 copy-start.1
  14.4 3.2 copy-start
  17.7 104.5 %all-to-all-start = ((f32[8,16,128,128]{3,2,1,0:T(8,128)}), f32[8,16,128,128]{3,2,1,0:T(8,128)}, u32[]{:S(2)}, u32[]{:S(2)}) async-start(f32[8,16,128,128]{3,2,1,0:T(8,128)} %copy-done), calls=%async_computation | async-start | bytes 16777216 | tf_op jit(solution)/shard_map/all_to_all | solution.py:387
  22.7 293.5 %reduce-scatter.2.cloned.1.call-start = ((), (), s32[]{:S(2)}) async-start(), calls=%async_computation.2 | async-start | bytes 9732096 | tf_op jit(solution)/shard_map/reduce_scatter | solution.py:417
  22.9 2.2 copy-start.2
  25.1 2.2 copy-start.4
  122.2 2.2 copy-start.3
Sparse Core Ops, SparseCore 0:
  154.4 72.8 reduce-scatter.1

commit v2 on v1

--- a/solution.py
+++ b/solution.py
@@ -62,7 +62,7 @@
             jax.ShapeDtypeStruct((pa_count, qblocks, BLOCK, BLOCK), jnp.float32),
             jax.ShapeDtypeStruct((8, query_count), jnp.float32),
         ],
-        compiler_params=pltpu.CompilerParams(vmem_limit_bytes=40 * MIB),
+        compiler_params=pltpu.CompilerParams(vmem_limit_bytes=56 * MIB),
         cost_estimate=pl.CostEstimate(
             flops=6 * teacher.size,
             bytes_accessed=4 * (teacher.size + pa_count * qblocks * BLOCK * BLOCK),
@@ -106,7 +106,7 @@
             jax.ShapeDtypeStruct((query_count, passage_count), jnp.float32),
             jax.ShapeDtypeStruct((8, query_count), jnp.float32),
         ],
-        compiler_params=pltpu.CompilerParams(vmem_limit_bytes=40 * MIB),
+        compiler_params=pltpu.CompilerParams(vmem_limit_bytes=56 * MIB),
         cost_estimate=pl.CostEstimate(
             flops=2 * query_count * passage_count * depth,
             bytes_accessed=4 * query_count * passage_count
@@ -144,7 +144,11 @@
         hard_parts.append(
             jnp.sum(
                 lax.fori_loop(
-                    0, pa_count, one_source, jnp.zeros((BLOCK, BLOCK), jnp.float32)
+                    0,
+                    pa_count,
+                    one_source,
+                    jnp.zeros((BLOCK, BLOCK), jnp.float32),
+                    unroll=4,
                 ),
                 axis=1,
                 keepdims=True,
@@ -191,7 +195,7 @@
             jax.ShapeDtypeStruct((pblocks, query_count, BLOCK), jnp.bfloat16),
             jax.ShapeDtypeStruct((pa_count, chunk_rows + 8, depth), jnp.float32),
         ],
-        compiler_params=pltpu.CompilerParams(vmem_limit_bytes=48 * MIB),
+        compiler_params=pltpu.CompilerParams(vmem_limit_bytes=56 * MIB),
         cost_estimate=pl.CostEstimate(
             flops=2 * query_count * passage_count * depth,
             bytes_accessed=6 * query_count * passage_count + 4 * query_count * depth,
@@ -295,11 +299,12 @@
         def _():
             down(m).start()
 
-    @pl.loop(0, blocks)
-    def _(k):
-        upper = blocks - 1 - k
-
-        @pl.when((me > 0) & (upper // share >= me))
+    @pl.loop(0, blocks + count - 2)
+    def _(step):
+        from_low = step - (me - 1)
+        upper = blocks - 1 - from_low
+
+        @pl.when((me > 0) & (from_low >= 0) & (upper // share >= me) & (upper >= 0))
         def _():
             up(upper).wait_recv()
             acc[upper] += from_below[upper]
@@ -308,14 +313,16 @@
             def _():
                 up(upper).start()
 
-        @pl.when((me < count - 1) & (k // share <= me))
-        def _():
-            down(k).wait_recv()
-            acc[k] += from_above[k]
-
-            @pl.when(k // share < me)
+        lower = step - (count - 2 - me)
+
+        @pl.when((me < count - 1) & (lower >= 0) & (lower // share <= me))
+        def _():
+            down(lower).wait_recv()
+            acc[lower] += from_above[lower]
+
+            @pl.when(lower // share < me)
             def _():
-                down(k).start()
+                down(lower).start()
 
     for c in range(share):
         out_ref[c * BLOCK : (c + 1) * BLOCK, :] = acc[me * share + c]
@@ -354,7 +361,7 @@
             pltpu.SemaphoreType.DMA((blocks,)),
         ],
         compiler_params=pltpu.CompilerParams(
-            collective_id=0, has_side_effects=True, vmem_limit_bytes=48 * MIB
+            collective_id=0, has_side_effects=True, vmem_limit_bytes=56 * MIB
         ),
         cost_estimate=pl.CostEstimate(
             flops=2 * query_count * blocks * BLOCK * depth,

time: 332 us -> 308 us (0.928)
  Pallas kernels: 210 us -> 195 us
  local copies, waits for them, and re-layouts: 17.2 us -> 9.51 us
    pallas_call x1, Pallas kernels: 162 us -> 143 us  [passage_gradient(): pl.pallas_call(functools.partial(passages_kernel, count), in_specs=[pl.Bl...]
    unnamed x11 -> x3, local copies, waits for them, and re-layouts: 13.3 us -> 3.16 us
    pallas_call x1, Pallas kernels: 4.04 us -> 9.48 us  [pack(): pl.pallas_call(pack_kernel, grid_spec=pltpu.PrefetchScalarGridSpec(num_sc...]
    pallas_call x1, Pallas kernels: 29.9 us -> 25.5 us  [dscore_and_query_part(): pl.pallas_call(functools.partial(dscore_kernel, scale), grid_spec=pltpu.P...]
  transfers between devices with their start and end apart: 2 -> 2, of which waited for: 0 -> 0; matrix products, arithmetic and copies ran while one was open for 0% -> 1% of each run, Pallas kernels for 54% -> 52%
where the time goes in v2:
time: 308 us; the launch traced here: 307 us
  Pallas kernels  195 us (63%)
  blocking collectives  80.3 us (26%)
  between operations  14.2 us (5%)
  local copies, waits for them, and re-layouts  9.51 us (3%)
  starting transfers between devices  5.14 us (2%)
    pallas_call x1, Pallas kernels, passage_gradient(): pl.pallas_call(functools.partial(passages_kernel, count), in_specs=[pl.Bl...  143 us
    all_gather x1, blocking collectives, per_device(): every = lax.all_gather(mine, 'pa')  80.3 us
    pallas_call x1, Pallas kernels, dscore_and_query_part(): pl.pallas_call(functools.partial(dscore_kernel, scale), grid_spec=pltpu.P...  25.5 us
    pallas_call x1, Pallas kernels, score_stats(): pl.pallas_call(functools.partial(scores_kernel, score_scale), grid=(query...  16.9 us
    pallas_call x1, Pallas kernels, pack(): pl.pallas_call(pack_kernel, grid_spec=pltpu.PrefetchScalarGridSpec(num_sc...  9.48 us
  transfers between devices with their start and end apart: 2, of which 0 were waited for; matrix products, arithmetic and copies ran while one was open for 1% of the time, Pallas kernels for 52%

profile of v2, /device:TPU:16, one launch (start us, length us, event | category | flops | bytes accessed | tf_op | source)
XLA Modules:
  0.0 307.0 jit_solution(10574452970287685820)
XLA Ops:
  7.2 0.8 add_select_fusion.2
  7.9 0.1 copy.29
  8.0 0.1 select_reduce_fusion
  8.1 0.7 copy.30.pick_ref
  8.8 9.5 %pack.1 = (f32[8,16,128,128]{3,2,1,0:T(8,128)}, f32[8,2048]{1,0:T(8,128)}) custom-call(s32[8,16]{1,0:T(8,128)} %copy.30.pick_ref, f32[2048,512]{1,0:T(8,128)} %teacher_ref.1), custom_call_target="tpu_custom_call" | custom-call | flops 6291456 | bytes 12582912 | tf_op jit(solution)/shard_map/pack/pallas_call | solution.py:48
  18.3 0.0 copy-start
  18.3 5.1 %all-to-all-start = ((f32[8,16,128,128]{3,2,1,0:T(8,128)}), f32[8,16,128,128]{3,2,1,0:T(8,128)}, u32[]{:S(2)}, u32[]{:S(2)}) async-start(f32[8,16,128,128]{3,2,1,0:T(8,128)} %get-tuple-element.12), calls=%async_computation | async-start | bytes 16777216 | tf_op jit(solution)/shard_map/all_to_all | solution.py:394
  23.4 0.0 reduce-scatter.2.cloned.1.call-start
  23.4 0.1 copy.31
  23.5 0.1 reshape.57
  23.6 0.0 copy-done
  23.6 16.9 %score_stats.1 = (f32[2048,2048]{1,0:T(8,128)}, f32[8,2048]{1,0:T(8,128)}) custom-call(bf16[2048,1024]{1,0:T(8,128)(2,1)} %queries_hbm.1, bf16[2048,1024]{1,0:T(8,128)(2,1)} %passages_ref.3), custom_call_target="tpu_custom_call" | custom-call | flops 8589934592 | bytes 25165824 | tf_op jit(solution)/shard_map/score_stats/pallas_call | solution.py:94
  40.5 0.8 slice.34
  41.4 80.3 %all-gather.1 = f32[8,6,2048]{2,1,0:T(8,128)S(1)} all-gather(f32[1,6,2048]{2,1,0:T(8,128)S(1)} %fusion), channel_id=2, replica_groups=mesh['pb'=4,'pa'=8] {'pa'}, dimensions={0}, use_global_device_ids=true | all-gather | bytes 442368 | tf_op jit(solution)/shard_map/all_gather | solution.py:402
  121.7 0.1 copy.36
  121.8 0.1 fusion.10
  121.9 0.1 copy.37
  122.0 0.3 slice_reduce_fusion.1
  122.3 0.1 fusion.4
  122.5 1.3 copy.38.lse_ref
  123.8 0.6 broadcast_add_fusion.col_ref
  124.4 0.0 all-to-all-done.tiles_ref
  124.4 25.5 %dscore.1 = (bf16[16,2048,128]{2,1,0:T(8,128)(2,1)}, f32[8,264,1024]{2,1,0:T(8,128)}) custom-call(s32[8,16]{1,0:T(8,128)} %broadcast_add_fusion.col_ref, f32[2048,2048]{1,0:T(8,128)} %get-tuple-element.11.scores_ref, f32[2048,2]{1,0:T(8,128)} %copy.38.lse_ref, f32[8,16,128,128]{3,2,1,0:T(8,128)} %all-to-all-done.tiles_ref, bf16[2048,1024]{1,0:T(8,128)(2,1)} %passages_ref.3), custom_call_target="tpu_custom_call" | custom-call | flops 8589934592 | bytes 33554432 | tf_op jit(solution)/shard_map/dscore/pallas_call | solution.py:175
  149.9 0.0 reduce-scatter.2.cloned.1.call-update
  150.0 0.1 fusion.6
  150.1 143.2 %passage_gradient.1 = f32[512,1024]{1,0:T(8,128)} custom-call(bf16[16,2048,128]{2,1,0:T(8,128)(2,1)} %get-tuple-element.14.dscore_hbm, bf16[2048,1024]{1,0:T(8,128)(2,1)} %queries_hbm.1), custom_call_target="tpu_custom_call" | custom-call | flops 8589934592 | bytes 209715200 | tf_op jit(solution)/shard_map/passage_gradient/pallas_call | solution.py:345
  293.3 0.0 reduce-scatter.2.cloned.1.call-done
  293.3 0.8 slice.51
  294.0 0.6 fusion.14
  294.7 2.3 slice_bitcast_fusion
  297.0 3.2 %copy.69 = f32[512,1024]{1,0:T(8,128)} copy(f32[512,1024]{1,0:T(8,128)} %passage_gradient.1) | data formatting | bytes 4194304
  (8 shorter events, 0.1 us)
Async XLA Ops:
  18.3 5.3 %copy-start = (f32[8,2048]{1,0:T(8,128)S(1)}, f32[8,2048]{1,0:T(8,128)}, u32[]{:S(2)}) copy-start(f32[8,2048]{1,0:T(8,128)} %get-tuple-element.10) | copy-start | bytes 196612
  18.3 106.1 %all-to-all-start = ((f32[8,16,128,128]{3,2,1,0:T(8,128)}), f32[8,16,128,128]{3,2,1,0:T(8,128)}, u32[]{:S(2)}, u32[]{:S(2)}) async-start(f32[8,16,128,128]{3,2,1,0:T(8,128)} %get-tuple-element.12), calls=%async_computation | async-start | bytes 16777216 | tf_op jit(solution)/shard_map/all_to_all | solution.py:394
  23.4 269.9 %reduce-scatter.2.cloned.1.call-start = ((), (), s32[]{:S(2)}) async-start(), calls=%async_computation.2 | async-start | bytes 9732096 | tf_op jit(solution)/shard_map/reduce_scatter | solution.py:424
Sparse Core Ops, SparseCore 0:
  150.1 72.7 reduce-scatter.1

commit v3 on v2

--- a/solution.py
+++ b/solution.py
@@ -118,13 +118,11 @@
 
 
 def dscore_kernel(
-    scale, col_ref, scores_ref, lse_ref, tiles_ref, passages_ref, dscore_ref, part_ref, weights
+    scale, col_ref, scores_ref, lse_ref, tiles_ref, dscore_ref, hard_ref, weights
 ):
     step = pl.program_id(0)
     rows, passage_count = scores_ref.shape
     pa_count = tiles_ref.shape[0]
-    chunks, chunk_rows, depth = part_ref.shape
-    chunk_rows -= 8
     weights[...] = scale * jnp.exp(scores_ref[...] - lse_ref[:, 0:1])
     hard_parts = []
     for half in range(rows // BLOCK):
@@ -154,24 +152,13 @@
                 keepdims=True,
             )
         )
-    hard = rows_to_lanes((jnp.concatenate(hard_parts, axis=0),), rows)
-    dscore = weights[...].astype(jnp.bfloat16)
-    for m in range(passage_count // BLOCK):
-        dscore_ref[m] = dscore[:, m * BLOCK : (m + 1) * BLOCK]
-    part = jnp.dot(dscore, passages_ref[...], preferred_element_type=jnp.float32)
-    for chunk in range(chunks):
-        part_ref[chunk, 0:chunk_rows, :] = part[chunk * chunk_rows : (chunk + 1) * chunk_rows]
-        part_ref[chunk, chunk_rows : chunk_rows + 8, :] = jnp.zeros((8, depth), jnp.float32)
-        part_ref[chunk, chunk_rows : chunk_rows + 8, 0:rows] = hard
-
-
-def dscore_and_query_part(scores, lse, tiles, cols, passages, scale):
+    hard_ref[...] = rows_to_lanes((jnp.concatenate(hard_parts, axis=0),), rows)
+    dscore_ref[...] = weights[...].astype(jnp.bfloat16)
+
+
+def dscore_and_hard(scores, lse, tiles, cols, scale):
     query_count, passage_count = scores.shape
-    depth = passages.shape[1]
     pa_count, qblocks = cols.shape
-    chunk_rows = query_count // pa_count
-    chunks = ROWS // chunk_rows
-    pblocks = passage_count // BLOCK
     return pl.pallas_call(
         functools.partial(dscore_kernel, scale),
         grid_spec=pltpu.PrefetchScalarGridSpec(
@@ -183,55 +170,70 @@
                 pl.BlockSpec(
                     (pa_count, ROWS // BLOCK, BLOCK, BLOCK), lambda i, cols: (0, i, 0, 0)
                 ),
-                pl.BlockSpec((passage_count, depth), lambda i, cols: (0, 0)),
             ],
             out_specs=[
-                pl.BlockSpec((pblocks, ROWS, BLOCK), lambda i, cols: (0, i, 0)),
-                pl.BlockSpec((chunks, chunk_rows + 8, depth), lambda i, cols: (i, 0, 0)),
+                pl.BlockSpec((ROWS, passage_count), lambda i, cols: (i, 0)),
+                pl.BlockSpec((8, ROWS), lambda i, cols: (0, i)),
             ],
             scratch_shapes=[pltpu.VMEM((ROWS, passage_count), jnp.float32)],
         ),
         out_shape=[
-            jax.ShapeDtypeStruct((pblocks, query_count, BLOCK), jnp.bfloat16),
-            jax.ShapeDtypeStruct((pa_count, chunk_rows + 8, depth), jnp.float32),
+            jax.ShapeDtypeStruct((query_count, passage_count), jnp.bfloat16),
+            jax.ShapeDtypeStruct((8, query_count), jnp.float32),
         ],
         compiler_params=pltpu.CompilerParams(vmem_limit_bytes=56 * MIB),
         cost_estimate=pl.CostEstimate(
-            flops=2 * query_count * passage_count * depth,
-            bytes_accessed=6 * query_count * passage_count + 4 * query_count * depth,
+            flops=4 * query_count * passage_count,
+            bytes_accessed=8 * query_count * passage_count,
             transcendentals=query_count * passage_count,
         ),
         name="dscore",
-    )(cols, scores, lse, tiles, passages)
-
-
-def passages_kernel(
+    )(cols, scores, lse, tiles)
+
+
+def gradients_kernel(
     count,
+    pa_count,
+    hard_ref,
     dscore_hbm,
     queries_hbm,
-    out_ref,
+    passages_hbm,
+    passage_out,
+    query_out,
+    hard_out,
     dscore,
     queries,
+    passages,
     acc,
-    from_below,
-    from_above,
+    landed,
+    part,
+    part_landed,
     load_sem,
     queries_sem,
+    passages_sem,
     up_send,
     up_recv,
     down_send,
     down_recv,
+    part_send,
+    part_recv,
 ):
     me = lax.axis_index("pb")
-    blocks = dscore.shape[0]
+    column = lax.axis_index("pa")
+    blocks = acc.shape[0]
     share = blocks // count
+    depth = queries.shape[1]
+    rows = query_out.shape[0]
     low = me < count // 2
 
     def in_order(k):
         return jnp.where(low, blocks - 1 - k, k)
 
     def load(m):
-        return pltpu.make_async_copy(dscore_hbm.at[m], dscore.at[m], load_sem.at[m])
+        place = pl.ds(pl.multiple_of(m * BLOCK, BLOCK), BLOCK)
+        return pltpu.make_async_copy(
+            dscore_hbm.at[:, place], dscore.at[:, place], load_sem.at[m]
+        )
 
     load_queries = pltpu.make_async_copy(queries_hbm, queries, queries_sem)
     load_queries.start()
@@ -239,6 +241,9 @@
     @pl.loop(0, blocks)
     def _(k):
         load(in_order(k)).start()
+
+    load_passages = pltpu.make_async_copy(passages_hbm, passages, passages_sem)
+    load_passages.start()
 
     barrier = pltpu.get_barrier_semaphore()
 
@@ -254,14 +259,24 @@
             barrier, inc=1, device_id={"pb": me + 1}, device_id_type=pl.DeviceIdType.MESH
         )
 
+    @pl.loop(1, pa_count)
+    def _(k):
+        pl.semaphore_signal(
+            barrier,
+            inc=1,
+            device_id={"pa": lax.rem(column + k, pa_count)},
+            device_id_type=pl.DeviceIdType.MESH,
+        )
+
     pl.semaphore_wait(
-        barrier, jnp.where(me > 0, 1, 0) + jnp.where(me < count - 1, 1, 0)
+        barrier,
+        pa_count - 1 + jnp.where(me > 0, 1, 0) + jnp.where(me < count - 1, 1, 0),
     )
 
     def up(m):
         return pltpu.make_async_remote_copy(
             src_ref=acc.at[m],
-            dst_ref=from_below.at[m],
+            dst_ref=landed.at[m + share],
             send_sem=up_send.at[m],
             recv_sem=up_recv.at[m],
             device_id={"pb": me + 1},
@@ -271,10 +286,30 @@
     def down(m):
         return pltpu.make_async_remote_copy(
             src_ref=acc.at[m],
-            dst_ref=from_above.at[m],
+            dst_ref=landed.at[m],
             send_sem=down_send.at[m],
             recv_sem=down_recv.at[m],
             device_id={"pb": me - 1},
+            device_id_type=pl.DeviceIdType.MESH,
+        )
+
+    def share_part(target, slot):
+        return pltpu.make_async_remote_copy(
+            src_ref=part.at[target],
+            dst_ref=part_landed.at[column],
+            send_sem=part_send.at[target],
+            recv_sem=part_recv.at[slot],
+            device_id={"pa": target},
+            device_id_type=pl.DeviceIdType.MESH,
+        )
+
+    def part_from(source):
+        return pltpu.make_async_remote_copy(
+            src_ref=part.at[source],
+            dst_ref=part_landed.at[source],
+            send_sem=part_send.at[source],
+            recv_sem=part_recv.at[source],
+            device_id={"pa": source},
             device_id_type=pl.DeviceIdType.MESH,
         )
 
@@ -285,7 +320,7 @@
         m = in_order(k)
         load(m).wait()
         acc[m] = lax.dot_general(
-            dscore[m],
+            dscore[:, pl.ds(pl.multiple_of(m * BLOCK, BLOCK), BLOCK)],
             queries[...],
             (((0,), (0,)), ((), ())),
             preferred_element_type=jnp.float32,
@@ -298,6 +333,24 @@
         @pl.when((me == count - 1) & (m // share < me))
         def _():
             down(m).start()
+
+    load_passages.wait()
+
+    @pl.loop(1, pa_count + 1)
+    def _(k):
+        target = lax.rem(column + k, pa_count)
+        part[target, 0:rows, :] = jnp.dot(
+            dscore[pl.ds(pl.multiple_of(target * rows, rows), rows), :],
+            passages[...],
+            preferred_element_type=jnp.float32,
+        )
+        part[target, rows : rows + 8, :] = jnp.zeros((8, depth), jnp.float32)
+        group = pl.multiple_of(target * rows // ROWS * ROWS, ROWS)
+        part[target, rows : rows + 8, 0:ROWS] = hard_ref[:, pl.ds(group, ROWS)]
+
+        @pl.when(k < pa_count)
+        def _():
+            share_part(target, column).start()
 
     @pl.loop(0, blocks + count - 2)
     def _(step):
@@ -307,7 +360,7 @@
         @pl.when((me > 0) & (from_low >= 0) & (upper // share >= me) & (upper >= 0))
         def _():
             up(upper).wait_recv()
-            acc[upper] += from_below[upper]
+            acc[upper] += landed[upper + share]
 
             @pl.when(upper // share > me)
             def _():
@@ -318,14 +371,29 @@
         @pl.when((me < count - 1) & (lower >= 0) & (lower // share <= me))
         def _():
             down(lower).wait_recv()
-            acc[lower] += from_above[lower]
+            acc[lower] += landed[lower]
 
             @pl.when(lower // share < me)
             def _():
                 down(lower).start()
 
     for c in range(share):
-        out_ref[c * BLOCK : (c + 1) * BLOCK, :] = acc[me * share + c]
+        passage_out[c * BLOCK : (c + 1) * BLOCK, :] = acc[me * share + c]
+
+    query_out[...] = part[column, 0:rows, :]
+    hard_out[...] = part[column, rows : rows + 8, 0:ROWS]
+
+    @pl.loop(1, pa_count)
+    def _(k):
+        source = lax.rem(column + pa_count - k, pa_count)
+        part_from(source).wait_recv()
+        query_out[...] += part_landed[source, 0:rows, :]
+        hard_out[...] += part_landed[source, rows : rows + 8, 0:ROWS]
+
+    @pl.loop(1, pa_count)
+    def _(k):
+        target = lax.rem(column + k, pa_count)
+        share_part(target, column).wait_send()
 
     @pl.loop(0, blocks)
     def _(m):
@@ -338,38 +406,51 @@
             down(m).wait_send()
 
 
-def passage_gradient(dscore, queries, count):
-    blocks, query_count, _ = dscore.shape
-    depth = queries.shape[1]
-    rows = blocks // count * BLOCK
+def gradients(hard, dscore, queries, passages, count, pa_count):
+    query_count, depth = queries.shape
+    passage_count = passages.shape[0]
+    blocks = passage_count // BLOCK
+    share = blocks // count
+    rows = query_count // pa_count
+    dma = pltpu.SemaphoreType.DMA
     return pl.pallas_call(
-        functools.partial(passages_kernel, count),
-        in_specs=[pl.BlockSpec(memory_space=pl.ANY)] * 2,
-        out_specs=pl.BlockSpec(memory_space=pltpu.VMEM),
-        out_shape=jax.ShapeDtypeStruct((rows, depth), jnp.float32),
+        functools.partial(gradients_kernel, count, pa_count),
+        in_specs=[pl.BlockSpec(memory_space=pltpu.VMEM)]
+        + [pl.BlockSpec(memory_space=pl.ANY)] * 3,
+        out_specs=[pl.BlockSpec(memory_space=pltpu.VMEM)] * 3,
+        out_shape=[
+            jax.ShapeDtypeStruct((share * BLOCK, depth), jnp.float32),
+            jax.ShapeDtypeStruct((rows, depth), jnp.float32),
+            jax.ShapeDtypeStruct((8, ROWS), jnp.float32),
+        ],
         scratch_shapes=[
-            pltpu.VMEM((blocks, query_count, BLOCK), jnp.bfloat16),
+            pltpu.VMEM((query_count, passage_count), jnp.bfloat16),
             pltpu.VMEM((query_count, depth), jnp.bfloat16),
+            pltpu.VMEM((passage_count, depth), jnp.bfloat16),
             pltpu.VMEM((blocks, BLOCK, depth), jnp.float32),
-            pltpu.VMEM((blocks, BLOCK, depth), jnp.float32),
-            pltpu.VMEM((blocks, BLOCK, depth), jnp.float32),
-            pltpu.SemaphoreType.DMA((blocks,)),
-            pltpu.SemaphoreType.DMA,
-            pltpu.SemaphoreType.DMA((blocks,)),
-            pltpu.SemaphoreType.DMA((blocks,)),
-            pltpu.SemaphoreType.DMA((blocks,)),
-            pltpu.SemaphoreType.DMA((blocks,)),
+            pltpu.VMEM((blocks + share, BLOCK, depth), jnp.float32),
+            pltpu.VMEM((pa_count, rows + 8, depth), jnp.float32),
+            pltpu.VMEM((pa_count, rows + 8, depth), jnp.float32),
+            dma((blocks,)),
+            dma,
+            dma,
+            dma((blocks,)),
+            dma((blocks,)),
+            dma((blocks,)),
+            dma((blocks,)),
+            dma((pa_count,)),
+            dma((pa_count,)),
         ],
         compiler_params=pltpu.CompilerParams(
-            collective_id=0, has_side_effects=True, vmem_limit_bytes=56 * MIB
+            collective_id=0, has_side_effects=True, vmem_limit_bytes=60 * MIB
         ),
         cost_estimate=pl.CostEstimate(
-            flops=2 * query_count * blocks * BLOCK * depth,
+            flops=4 * query_count * passage_count * depth,
             bytes_accessed=200 * MIB,
             transcendentals=0,
         ),
-        name="passage_gradient",
-    )(dscore, queries)
+        name="gradients",
+    )(hard, dscore, queries, passages)
 
 
 def per_device(queries, passages, teacher, block_ids):
@@ -418,16 +499,12 @@
     )
     lse = jnp.stack([lse_student, lse_teacher], axis=1)
 
-    dscore, query_part = dscore_and_query_part(
-        scores, lse, tiles, cols, passages, loss_scale * score_scale
-    )
-    summed = lax.psum_scatter(query_part, "pa", scatter_dimension=0, tiled=False)
-    grad_passages = passage_gradient(dscore, queries, pb_count)
+    dscore, hard_part = dscore_and_hard(scores, lse, tiles, cols, loss_scale * score_scale)
+    grad_passages, grad_queries, hard_rows = gradients(
+        hard_part, dscore, queries, passages, pb_count, pa_count
+    )
     row_count = query_count // pa_count
-    grad_queries = summed[0:row_count]
-    hard = lax.dynamic_slice_in_dim(
-        summed[row_count], me * row_count % ROWS, row_count
-    )
+    hard = lax.dynamic_slice_in_dim(hard_rows[0], me * row_count % ROWS, row_count)
     loss_rows = (
         lax.dynamic_slice_in_dim(lse_student + teacher_part, me * row_count, row_count) - hard
     )

time: 308 us -> 289 us (0.938)
  between operations: 14.2 us -> 0.74 us
  Pallas kernels: 195 us -> 190 us
    pallas_call x2, Pallas kernels: 169 us -> 163 us  [the longest x1 146 us: gradients(): pl.pallas_call(functools.partial(gradients_kernel, count, pa_count), in_s...]
  transfers between devices with their start and end apart: 2 -> 1, of which waited for: 0 -> 0; matrix products, arithmetic and copies ran while one was open for 1% -> 1% of each run, Pallas kernels for 52% -> 6%
where the time goes in v3:
time: 289 us; the launch traced here: 288 us
  Pallas kernels  190 us (66%)
  blocking collectives  80.4 us (28%)
  local copies, waits for them, and re-layouts  9.45 us (3%)
  starting transfers between devices  5.17 us (2%)
    pallas_call x1, Pallas kernels, gradients(): pl.pallas_call(functools.partial(gradients_kernel, count, pa_count), in_s...  146 us
    all_gather x1, blocking collectives, per_device(): every = lax.all_gather(mine, 'pa')  80.4 us
    pallas_call x1, Pallas kernels, dscore_and_hard(): pl.pallas_call(functools.partial(dscore_kernel, scale), grid_spec=pltpu.P...  17.8 us
    pallas_call x1, Pallas kernels, score_stats(): pl.pallas_call(functools.partial(scores_kernel, score_scale), grid=(query...  16.9 us
    pallas_call x1, Pallas kernels, pack(): pl.pallas_call(pack_kernel, grid_spec=pltpu.PrefetchScalarGridSpec(num_sc...  9.47 us
  transfers between devices with their start and end apart: 1, of which 0 were waited for; matrix products, arithmetic and copies ran while one was open for 1% of the time, Pallas kernels for 6%

profile of v3, /device:TPU:16, one launch (start us, length us, event | category | flops | bytes accessed | tf_op | source)
XLA Modules:
  0.0 288.2 jit_solution(7116045345256359693)
XLA Ops:
  0.6 0.8 add_select_fusion.2
  1.4 0.1 copy.29
  1.5 0.1 select_reduce_fusion
  1.6 0.7 copy.30.pick_ref
  2.2 9.5 %pack.1 = (f32[8,16,128,128]{3,2,1,0:T(8,128)}, f32[8,2048]{1,0:T(8,128)}) custom-call(s32[8,16]{1,0:T(8,128)} %copy.30.pick_ref, f32[2048,512]{1,0:T(8,128)} %teacher_ref.1), custom_call_target="tpu_custom_call" | custom-call | flops 6291456 | bytes 12582912 | tf_op jit(solution)/shard_map/pack/pallas_call | solution.py:48
  11.7 0.0 copy-start
  11.7 5.2 %all-to-all-start = ((f32[8,16,128,128]{3,2,1,0:T(8,128)}), f32[8,16,128,128]{3,2,1,0:T(8,128)}, u32[]{:S(2)}, u32[]{:S(2)}) async-start(f32[8,16,128,128]{3,2,1,0:T(8,128)} %get-tuple-element.15), calls=%async_computation | async-start | bytes 16777216 | tf_op jit(solution)/shard_map/all_to_all | solution.py:475
  16.9 0.1 copy.31
  17.0 0.1 reshape.53
  17.1 0.0 copy-done
  17.1 16.9 %score_stats.1 = (f32[2048,2048]{1,0:T(8,128)}, f32[8,2048]{1,0:T(8,128)}) custom-call(bf16[2048,1024]{1,0:T(8,128)(2,1)} %queries_hbm.1, bf16[2048,1024]{1,0:T(8,128)(2,1)} %passages_hbm.1), custom_call_target="tpu_custom_call" | custom-call | flops 8589934592 | bytes 25165824 | tf_op jit(solution)/shard_map/score_stats/pallas_call | solution.py:94
  34.0 0.8 slice.27
  34.9 80.4 %all-gather.1 = f32[8,6,2048]{2,1,0:T(8,128)S(1)} all-gather(f32[1,6,2048]{2,1,0:T(8,128)S(1)} %fusion), channel_id=2, replica_groups=mesh['pb'=4,'pa'=8] {'pa'}, dimensions={0}, use_global_device_ids=true | all-gather | bytes 442368 | tf_op jit(solution)/shard_map/all_gather | solution.py:483
  115.3 0.1 copy.36
  115.4 0.1 fusion.10
  115.5 0.1 copy.37
  115.5 0.3 slice_reduce_fusion.1
  115.8 0.1 multiply_reduce_fusion
  115.9 0.1 fusion.4
  116.1 1.3 copy.38.lse_ref
  117.4 0.6 broadcast_add_fusion.col_ref
  118.0 0.0 all-to-all-done.tiles_ref
  118.0 17.8 %dscore.1 = (bf16[2048,2048]{1,0:T(8,128)(2,1)}, f32[8,2048]{1,0:T(8,128)}) custom-call(s32[8,16]{1,0:T(8,128)} %broadcast_add_fusion.col_ref, f32[2048,2048]{1,0:T(8,128)} %get-tuple-element.14.scores_ref, f32[2048,2]{1,0:T(8,128)} %copy.38.lse_ref, f32[8,16,128,128]{3,2,1,0:T(8,128)} %all-to-all-done.tiles_ref), custom_call_target="tpu_custom_call" | custom-call | flops 16777216 | bytes 33554432 | tf_op jit(solution)/shard_map/dscore/pallas_call | solution.py:162
  135.8 145.5 %gradients.1 = (f32[512,1024]{1,0:T(8,128)}, f32[256,1024]{1,0:T(8,128)}, f32[8,256]{1,0:T(8,128)}) custom-call(f32[8,2048]{1,0:T(8,128)} %get-tuple-element.16.hard_ref, bf16[2048,2048]{1,0:T(8,128)(2,1)} %get-tuple-element.17.dscore_hbm, bf16[2048,1024]{1,0:T(8,128)(2,1)} %queries_hbm.1, bf16[2048,1024]{1,0:T(8,128)(2,1)} %passages_hbm.1), custom_call_target="tpu_custom_call" | custom-call | flops 17179869184 | bytes 209715200 | tf_op jit(solution)/shard_map/gradients/pallas_call | solution.py:416
  281.4 0.7 slice.35
  282.1 0.6 fusion.14
  282.7 2.3 copy.70
  285.0 3.2 %copy.71 = f32[512,1024]{1,0:T(8,128)} copy(f32[512,1024]{1,0:T(8,128)} %get-tuple-element.37) | data formatting | bytes 4194304
  (7 shorter events, 0.1 us)
Async XLA Ops:
  11.7 5.4 %copy-start = (f32[8,2048]{1,0:T(8,128)S(1)}, f32[8,2048]{1,0:T(8,128)}, u32[]{:S(2)}) copy-start(f32[8,2048]{1,0:T(8,128)} %get-tuple-element.13) | copy-start | bytes 196612
  11.7 106.3 %all-to-all-start = ((f32[8,16,128,128]{3,2,1,0:T(8,128)}), f32[8,16,128,128]{3,2,1,0:T(8,128)}, u32[]{:S(2)}, u32[]{:S(2)}) async-start(f32[8,16,128,128]{3,2,1,0:T(8,128)} %get-tuple-element.15), calls=%async_computation | async-start | bytes 16777216 | tf_op jit(solution)/shard_map/all_to_all | solution.py:475

commit v4 on v3

--- a/solution.py
+++ b/solution.py
@@ -146,7 +146,7 @@
                     pa_count,
                     one_source,
                     jnp.zeros((BLOCK, BLOCK), jnp.float32),
-                    unroll=4,
+                    unroll=8,
                 ),
                 axis=1,
                 keepdims=True,
@@ -377,18 +377,20 @@
             def _():
                 down(lower).start()
 
+        @pl.when(step == max(blocks - share - 2, 0))
+        def _():
+            query_out[...] = part[column, 0:rows, :]
+            hard_out[...] = part[column, rows : rows + 8, 0:ROWS]
+
+            @pl.loop(1, pa_count)
+            def _(k):
+                source = lax.rem(column + pa_count - k, pa_count)
+                part_from(source).wait_recv()
+                query_out[...] += part_landed[source, 0:rows, :]
+                hard_out[...] += part_landed[source, rows : rows + 8, 0:ROWS]
+
     for c in range(share):
         passage_out[c * BLOCK : (c + 1) * BLOCK, :] = acc[me * share + c]
-
-    query_out[...] = part[column, 0:rows, :]
-    hard_out[...] = part[column, rows : rows + 8, 0:ROWS]
-
-    @pl.loop(1, pa_count)
-    def _(k):
-        source = lax.rem(column + pa_count - k, pa_count)
-        part_from(source).wait_recv()
-        query_out[...] += part_landed[source, 0:rows, :]
-        hard_out[...] += part_landed[source, rows : rows + 8, 0:ROWS]
 
     @pl.loop(1, pa_count)
     def _(k):

time: 289 us -> 287 us (level)
  no operation moved by 1% of the time
where the time goes in v4:
time: 287 us; the launch traced here: 286 us
  Pallas kernels  188 us (66%)
  blocking collectives  80.4 us (28%)
  local copies, waits for them, and re-layouts  9.45 us (3%)
  starting transfers between devices  5.17 us (2%)
    pallas_call x1, Pallas kernels, gradients(): pl.pallas_call(functools.partial(gradients_kernel, count, pa_count), in_s...  145 us
    all_gather x1, blocking collectives, per_device(): every = lax.all_gather(mine, 'pa')  80.4 us
    pallas_call x1, Pallas kernels, score_stats(): pl.pallas_call(functools.partial(scores_kernel, score_scale), grid=(query...  16.9 us
    pallas_call x1, Pallas kernels, dscore_and_hard(): pl.pallas_call(functools.partial(dscore_kernel, scale), grid_spec=pltpu.P...  16.6 us
    pallas_call x1, Pallas kernels, pack(): pl.pallas_call(pack_kernel, grid_spec=pltpu.PrefetchScalarGridSpec(num_sc...  9.48 us
  transfers between devices with their start and end apart: 1, of which 0 were waited for; matrix products, arithmetic and copies ran while one was open for 1% of the time, Pallas kernels for 6%

profile of v4, /device:TPU:16, one launch (start us, length us, event | category | flops | bytes accessed | tf_op | source)
XLA Modules:
  0.0 286.2 jit_solution(3789244034125515395)
XLA Ops:
  0.6 0.8 add_select_fusion.2
  1.4 0.1 copy.29
  1.5 0.1 select_reduce_fusion
  1.6 0.7 copy.30.pick_ref
  2.2 9.5 %pack.1 = (f32[8,16,128,128]{3,2,1,0:T(8,128)}, f32[8,2048]{1,0:T(8,128)}) custom-call(s32[8,16]{1,0:T(8,128)} %copy.30.pick_ref, f32[2048,512]{1,0:T(8,128)} %teacher_ref.1), custom_call_target="tpu_custom_call" | custom-call | flops 6291456 | bytes 12582912 | tf_op jit(solution)/shard_map/pack/pallas_call | solution.py:48
  11.7 0.0 copy-start
  11.7 5.2 %all-to-all-start = ((f32[8,16,128,128]{3,2,1,0:T(8,128)}), f32[8,16,128,128]{3,2,1,0:T(8,128)}, u32[]{:S(2)}, u32[]{:S(2)}) async-start(f32[8,16,128,128]{3,2,1,0:T(8,128)} %get-tuple-element.15), calls=%async_computation | async-start | bytes 16777216 | tf_op jit(solution)/shard_map/all_to_all | solution.py:477
  16.9 0.1 copy.31
  17.0 0.1 reshape.53
  17.1 0.0 copy-done
  17.1 16.9 %score_stats.1 = (f32[2048,2048]{1,0:T(8,128)}, f32[8,2048]{1,0:T(8,128)}) custom-call(bf16[2048,1024]{1,0:T(8,128)(2,1)} %queries_hbm.1, bf16[2048,1024]{1,0:T(8,128)(2,1)} %passages_hbm.1), custom_call_target="tpu_custom_call" | custom-call | flops 8589934592 | bytes 25165824 | tf_op jit(solution)/shard_map/score_stats/pallas_call | solution.py:94
  34.0 0.8 slice.27
  34.9 80.4 %all-gather.1 = f32[8,6,2048]{2,1,0:T(8,128)S(1)} all-gather(f32[1,6,2048]{2,1,0:T(8,128)S(1)} %fusion), channel_id=2, replica_groups=mesh['pb'=4,'pa'=8] {'pa'}, dimensions={0}, use_global_device_ids=true | all-gather | bytes 442368 | tf_op jit(solution)/shard_map/all_gather | solution.py:485
  115.3 0.1 copy.36
  115.4 0.1 fusion.10
  115.5 0.1 copy.37
  115.5 0.3 slice_reduce_fusion.1
  115.8 0.1 multiply_reduce_fusion
  115.9 0.1 fusion.4
  116.1 1.3 copy.38.lse_ref
  117.4 0.6 broadcast_add_fusion.col_ref
  118.0 0.0 all-to-all-done.tiles_ref
  118.0 16.6 %dscore.1 = (bf16[2048,2048]{1,0:T(8,128)(2,1)}, f32[8,2048]{1,0:T(8,128)}) custom-call(s32[8,16]{1,0:T(8,128)} %broadcast_add_fusion.col_ref, f32[2048,2048]{1,0:T(8,128)} %get-tuple-element.14.scores_ref, f32[2048,2]{1,0:T(8,128)} %copy.38.lse_ref, f32[8,16,128,128]{3,2,1,0:T(8,128)} %all-to-all-done.tiles_ref), custom_call_target="tpu_custom_call" | custom-call | flops 16777216 | bytes 33554432 | tf_op jit(solution)/shard_map/dscore/pallas_call | solution.py:162
  134.6 144.7 %gradients.1 = (f32[512,1024]{1,0:T(8,128)}, f32[256,1024]{1,0:T(8,128)}, f32[8,256]{1,0:T(8,128)}) custom-call(f32[8,2048]{1,0:T(8,128)} %get-tuple-element.16.hard_ref, bf16[2048,2048]{1,0:T(8,128)(2,1)} %get-tuple-element.17.dscore_hbm, bf16[2048,1024]{1,0:T(8,128)(2,1)} %queries_hbm.1, bf16[2048,1024]{1,0:T(8,128)(2,1)} %passages_hbm.1), custom_call_target="tpu_custom_call" | custom-call | flops 17179869184 | bytes 209715200 | tf_op jit(solution)/shard_map/gradients/pallas_call | solution.py:418
  279.4 0.7 slice.35
  280.1 0.6 fusion.14
  280.7 2.3 copy.70
  283.0 3.2 %copy.71 = f32[512,1024]{1,0:T(8,128)} copy(f32[512,1024]{1,0:T(8,128)} %get-tuple-element.37) | data formatting | bytes 4194304
  (7 shorter events, 0.1 us)
Async XLA Ops:
  11.7 5.4 %copy-start = (f32[8,2048]{1,0:T(8,128)S(1)}, f32[8,2048]{1,0:T(8,128)}, u32[]{:S(2)}) copy-start(f32[8,2048]{1,0:T(8,128)} %get-tuple-element.13) | copy-start | bytes 196612
  11.7 106.3 %all-to-all-start = ((f32[8,16,128,128]{3,2,1,0:T(8,128)}), f32[8,16,128,128]{3,2,1,0:T(8,128)}, u32[]{:S(2)}, u32[]{:S(2)}) async-start(f32[8,16,128,128]{3,2,1,0:T(8,128)} %get-tuple-element.15), calls=%async_computation | async-start | bytes 16777216 | tf_op jit(solution)/shard_map/all_to_all | solution.py:477
